TPU v7x, 256 devices: a whole 4x4x8 slice. The times are simulated.
256 devices in a mesh: leaf: 32 (over y, z), sub: 8 (over x, core).
Axes of the slice: x: 4, y: 4, z: 8, core: 2. Of those that a mesh axis runs over, the one named last changes fastest.
Arguments:
- rhs: float32 [8, 32, 1024, 128], P('sub', 'leaf'), may hold values from -6 to 6
- leaf_block: bfloat16 [8, 32, 1024, 1024], P('sub', 'leaf')
- leaf_inverse: bfloat16 [8, 32, 1024, 1024], P('sub', 'leaf')
- level_basis: float32 [8, 32, 5, 1024, 128], P('sub', 'leaf'), may hold values from -0.1875 to 0.1875
- level_core: float32 [8, 32, 5, 128, 128], P('sub', 'leaf')
- skeleton_basis: float32 [8, 32, 1024, 128], P('sub', 'leaf'), may hold values from -0.1875 to 0.1875
- coupling: float32 [8, 8, 128, 128], P('sub'), may hold values from -0.09375 to 0.09375
Outputs:
- solution: float32 [8, 32, 1024, 128], P('sub', 'leaf')
All inputs are finite; a program needn't handle non-finite values.
Results may differ from a plain program's by a relative error of at most 0.0003.
Values sent between devices are 32-bit elements; how exact they have to be, the bound alone decides.
A program may use at most 64 MiB of HBM per device.

v0:
```python
import jax
import jax.numpy as jnp
from jax import lax
from jax.sharding import PartitionSpec as P

ROUNDS = 2


HI = lax.Precision.HIGHEST


def partner(x, axis, stride):
    return lax.ppermute(x, axis, [(i, i ^ 1 << stride) for i in range(lax.axis_size(axis))])


def matmul(left, right):
    return jnp.dot(left, right, precision=HI, preferred_element_type=jnp.float32)


def tmatmul(left, right):
    return lax.dot_general(
        left, right, (((0,), (0,)), ((), ())), precision=HI, preferred_element_type=jnp.float32
    )


def group_sum(proj, level):
    total = proj
    for bit_num in range(level + 1):
        total = total + partner(total, "leaf", bit_num)
    return total


def inner_solve(field, inverse, basis, core):
    x = matmul(inverse, field)
    depth = lax.axis_size("leaf").bit_length() - 1
    for level in range(depth):
        proj = tmatmul(basis[level], x)
        group = group_sum(proj, level)
        x = x - matmul(basis[level], matmul(core[level], group))
    return x


def body(rhs, leaf_block, leaf_inverse, level_basis, level_core, skeleton_basis, coupling):
    target = rhs[0, 0]
    block = leaf_block[0, 0].astype(jnp.float32)
    inverse = leaf_inverse[0, 0].astype(jnp.float32)
    basis = level_basis[0, 0]
    core = level_core[0, 0]
    skeleton = skeleton_basis[0, 0]
    row_coupling = coupling[0]
    solution = inner_solve(target, inverse, basis, core)
    for outer in range(ROUNDS):
        local_skel = tmatmul(skeleton, solution)
        subtree_total = lax.psum(local_skel, "leaf")
        every_skel = lax.all_gather(subtree_total[None], "sub", axis=0, tiled=True)
        mixed = jnp.einsum(
            "tkj,tjr->kr",
            row_coupling,
            every_skel,
            precision=HI,
            preferred_element_type=jnp.float32,
        )
        applied = matmul(block, solution) + matmul(skeleton, mixed)
        solution = solution + inner_solve(target - applied, inverse, basis, core)
    return solution[None, None]


def solution(mesh):
    return jax.shard_map(
        body,
        mesh=mesh,
        in_specs=(
            P("sub", "leaf", None, None),
            P("sub", "leaf", None, None),
            P("sub", "leaf", None, None),
            P("sub", "leaf", None, None, None),
            P("sub", "leaf", None, None, None),
            P("sub", "leaf", None, None),
            P("sub", None, None, None),
        ),
        out_specs=P("sub", "leaf", None, None),
        check_vma=False,
    )
```

profile of v0, /device:TPU:6, one launch (start us, length us, event | category | flops | bytes accessed | tf_op | source)
XLA Modules:
  0.0 641.2 jit_solution(17399125690273079579)
XLA Ops:
  8.1 3.0 fusion.8
  22.8 3.4 collective-permute-start.2
  32.3 3.0 collective-permute-done.3
  40.6 7.6 %collective-permute-start.5 = (f32[128,128]{0,1:T(8,128)S(1)}, f32[128,128]{0,1:T(8,128)S(1)}, u32[]{:S(2)}, u32[]{:S(2)}) collective-permute-start(f32[128,128]{0,1:T(8,128)S(1)} %add.161), channel_id=1, source_target_pairs={{0,32},{8,40},{16,48},{24,56},{32,0},{40,8},{48,16},{56,24},{64,96... | collective-permute-start | bytes 196616 | tf_op jit(solution)/shard_map/ppermute | solution.py:13
  53.2 3.7 collective-permute-done.6
  58.4 5.2 collective-permute-done.7
  63.6 5.3 collective-permute-start.8
  68.9 2.9 collective-permute-done.8
  78.2 5.1 collective-permute-done.10
  84.4 4.1 collective-permute-done.11
  88.5 4.7 collective-permute-start.12
  93.3 3.5 collective-permute-done.12
  101.2 3.3 collective-permute-start.14
  109.6 139.8 %all-reduce.3.cloned.1.call-done = f32[1,128,128]{1,2,0:T(8,128)} async-done(((f32[1,128,128]{1,2,0:T(8,128)}), f32[1,128,128]{1,2,0:T(8,128)}) %all-reduce.3.cloned.1.call-update) | async-done | bytes 65552 | tf_op jit(solution)/shard_map/psum | solution.py:54
  250.4 13.6 %all_gather.6 = f32[8,128,128]{2,1,0:T(8,128)S(1)} all-gather(f32[1,128,128]{2,1,0:T(8,128)S(1)} %copy.30), channel_id=1, replica_groups=mesh['leaf'=32,'sub'=8] {'sub'}, dimensions={0}, use_global_device_ids=true | all-gather | bytes 589824 | tf_op jit(solution)/shard_map/all_gather | solution.py:55
  284.3 3.0 collective-permute-done.16
  288.8 3.7 collective-permute-done.17
  296.0 3.0 collective-permute-done.18
  301.1 3.1 collective-permute-done.19
  304.2 2.8 collective-permute-start.20
  307.0 5.5 collective-permute-done.20
  319.1 3.3 collective-permute-start.22
  322.4 2.9 collective-permute-done.22
  325.3 3.6 collective-permute-start.23
  328.9 4.8 collective-permute-done.23
  341.5 3.5 collective-permute-done.25
  347.7 3.3 collective-permute-done.26
  351.0 2.8 collective-permute-start.27
  353.8 6.2 collective-permute-done.27
  361.5 2.8 collective-permute-done.28
  366.8 3.3 collective-permute-done.29
  373.5 137.1 %all-reduce.5.cloned.1.call-done = f32[1,128,128]{1,2,0:T(8,128)} async-done(((f32[1,128,128]{1,2,0:T(8,128)}), f32[1,128,128]{1,2,0:T(8,128)}) %all-reduce.5.cloned.1.call-update) | async-done | bytes 65552 | tf_op jit(solution)/shard_map/psum | solution.py:54
  511.5 13.5 %all_gather.7 = f32[8,128,128]{2,1,0:T(8,128)S(1)} all-gather(f32[1,128,128]{2,1,0:T(8,128)S(1)} %copy.37), channel_id=1, replica_groups=mesh['leaf'=32,'sub'=8] {'sub'}, dimensions={0}, use_global_device_ids=true | all-gather | bytes 589824 | tf_op jit(solution)/shard_map/all_gather | solution.py:55
  527.6 2.9 fusion.30
  545.5 3.0 collective-permute-done.31
  550.0 3.7 collective-permute-done.32
  557.2 3.7 collective-permute-done.33
  562.5 5.1 collective-permute-done.34
  568.1 8.3 %collective-permute-done.35 = f32[128,128]{0,1:T(8,128)S(1)} collective-permute-done((f32[128,128]{0,1:T(8,128)S(1)}, f32[128,128]{0,1:T(8,128)S(1)}, u32[]{:S(2)}, u32[]{:S(2)}) %collective-permute-start.35) | collective-permute-done | bytes 65568 | tf_op jit(solution)/shard_map/ppermute | solution.py:13
  578.4 4.3 collective-permute-done.36
  583.4 5.2 collective-permute-done.37
  590.0 7.1 %collective-permute-done.38 = f32[128,128]{0,1:T(8,128)S(1)} collective-permute-done((f32[128,128]{0,1:T(8,128)S(1)}, f32[128,128]{0,1:T(8,128)S(1)}, u32[]{:S(2)}, u32[]{:S(2)}) %collective-permute-start.38) | collective-permute-done | bytes 65568 | tf_op jit(solution)/shard_map/ppermute | solution.py:13
  598.7 2.8 collective-permute-done.39
  603.6 4.1 collective-permute-done.40
  609.2 4.5 collective-permute-done.41
  615.1 6.9 %collective-permute-done.42 = f32[128,128]{0,1:T(8,128)S(1)} collective-permute-done((f32[128,128]{0,1:T(8,128)S(1)}, f32[128,128]{0,1:T(8,128)S(1)}, u32[]{:S(2)}, u32[]{:S(2)}) %collective-permute-start.42) | collective-permute-done | bytes 65568 | tf_op jit(solution)/shard_map/ppermute | solution.py:13
  623.5 2.8 collective-permute-done.43
  626.4 3.3 collective-permute-start.44
  (164 shorter events, 142.6 us)
Async XLA Ops:
  6.5 242.9 %all-reduce.3.cloned.1.call-start = ((), (), s32[]{:S(2)}) async-start(), calls=%async_computation | async-start | bytes 131072 | tf_op jit(solution)/shard_map/psum | solution.py:54
  12.1 4.4 collective-permute-start
  18.4 4.4 collective-permute-start.1
  22.8 5.6 collective-permute-start.2
  30.3 5.1 collective-permute-start.3
  35.3 5.3 collective-permute-start.4
  40.6 9.8 %collective-permute-start.5 = (f32[128,128]{0,1:T(8,128)S(1)}, f32[128,128]{0,1:T(8,128)S(1)}, u32[]{:S(2)}, u32[]{:S(2)}) collective-permute-start(f32[128,128]{0,1:T(8,128)S(1)} %add.161), channel_id=1, source_target_pairs={{0,32},{8,40},{16,48},{24,56},{32,0},{40,8},{48,16},{56,24},{64,96... | collective-permute-start | bytes 196616 | tf_op jit(solution)/shard_map/ppermute | solution.py:13
  52.3 4.6 collective-permute-start.6
  56.9 6.6 %collective-permute-start.7 = (f32[128,128]{0,1:T(8,128)S(1)}, f32[128,128]{0,1:T(8,128)S(1)}, u32[]{:S(2)}, u32[]{:S(2)}) collective-permute-start(f32[128,128]{0,1:T(8,128)S(1)} %add.163), channel_id=1, source_target_pairs={{0,16},{8,24},{16,0},{24,8},{32,48},{40,56},{48,32},{56,40},{64,80... | collective-permute-start | bytes 196616 | tf_op jit(solution)/shard_map/ppermute | solution.py:13
  63.6 8.3 %collective-permute-start.8 = (f32[128,128]{0,1:T(8,128)S(1)}, f32[128,128]{0,1:T(8,128)S(1)}, u32[]{:S(2)}, u32[]{:S(2)}) collective-permute-start(f32[128,128]{0,1:T(8,128)S(1)} %add.164), channel_id=1, source_target_pairs={{0,32},{8,40},{16,48},{24,56},{32,0},{40,8},{48,16},{56,24},{64,96... | collective-permute-start | bytes 196616 | tf_op jit(solution)/shard_map/ppermute | solution.py:13
  71.8 4.4 collective-permute-start.9
  78.1 5.2 collective-permute-start.10
  83.3 5.3 collective-permute-start.11
  88.5 8.3 %collective-permute-start.12 = (f32[128,128]{0,1:T(8,128)S(1)}, f32[128,128]{0,1:T(8,128)S(1)}, u32[]{:S(2)}, u32[]{:S(2)}) collective-permute-start(f32[128,128]{0,1:T(8,128)S(1)} %add.168), channel_id=1, source_target_pairs={{0,32},{8,40},{16,48},{24,56},{32,0},{40,8},{48,16},{56,24},{64,96... | collective-permute-start | bytes 196616 | tf_op jit(solution)/shard_map/ppermute | solution.py:13
  96.8 4.4 collective-permute-start.13
  101.2 5.9 collective-permute-start.14
  109.6 401.0 %all-reduce.5.cloned.1.call-start = ((), (), s32[]{:S(2)}) async-start(), calls=%async_computation.1 | async-start | bytes 131072 | tf_op jit(solution)/shard_map/psum | solution.py:54
  273.4 4.5 collective-permute-start.15
  282.9 4.4 collective-permute-start.16
  287.3 5.3 collective-permute-start.17
  294.4 4.5 collective-permute-start.18
  299.0 5.3 collective-permute-start.19
  304.2 8.3 %collective-permute-start.20 = (f32[128,128]{0,1:T(8,128)S(1)}, f32[128,128]{0,1:T(8,128)S(1)}, u32[]{:S(2)}, u32[]{:S(2)}) collective-permute-start(f32[128,128]{0,1:T(8,128)S(1)} %add.178), channel_id=1, source_target_pairs={{0,32},{8,40},{16,48},{24,56},{32,0},{40,8},{48,16},{56,24},{64,96... | collective-permute-start | bytes 196616 | tf_op jit(solution)/shard_map/ppermute | solution.py:13
  314.4 4.6 collective-permute-start.21
  319.1 6.3 collective-permute-start.22
  325.3 8.4 %collective-permute-start.23 = (f32[128,128]{0,1:T(8,128)S(1)}, f32[128,128]{0,1:T(8,128)S(1)}, u32[]{:S(2)}, u32[]{:S(2)}) collective-permute-start(f32[128,128]{0,1:T(8,128)S(1)} %add.181), channel_id=1, source_target_pairs={{0,32},{8,40},{16,48},{24,56},{32,0},{40,8},{48,16},{56,24},{64,96... | collective-permute-start | bytes 196616 | tf_op jit(solution)/shard_map/ppermute | solution.py:13
  333.7 4.4 collective-permute-start.24
  340.0 5.0 collective-permute-start.25
  345.0 6.0 collective-permute-start.26
  351.0 9.0 %collective-permute-start.27 = (f32[128,128]{0,1:T(8,128)S(1)}, f32[128,128]{0,1:T(8,128)S(1)}, u32[]{:S(2)}, u32[]{:S(2)}) collective-permute-start(f32[128,128]{0,1:T(8,128)S(1)} %add.185), channel_id=1, source_target_pairs={{0,32},{8,40},{16,48},{24,56},{32,0},{40,8},{48,16},{56,24},{64,96... | collective-permute-start | bytes 196616 | tf_op jit(solution)/shard_map/ppermute | solution.py:13
  359.9 4.4 collective-permute-start.28
  364.3 5.9 collective-permute-start.29
  373.5 154.1 %copy-start.8 = (f32[1024,128]{1,0:T(8,128)S(1)}, f32[1024,128]{1,0:T(8,128)}, u32[]{:S(2)}) copy-start(f32[1024,128]{1,0:T(8,128)} %copy-done.7) | copy-start | bytes 1572868
  534.6 4.5 collective-permute-start.30
  544.1 4.4 collective-permute-start.31
  548.5 5.3 collective-permute-start.32
  555.6 5.3 collective-permute-start.33
  560.9 6.7 %collective-permute-start.34 = (f32[128,128]{0,1:T(8,128)S(1)}, f32[128,128]{0,1:T(8,128)S(1)}, u32[]{:S(2)}, u32[]{:S(2)}) collective-permute-start(f32[128,128]{0,1:T(8,128)S(1)} %add.195), channel_id=1, source_target_pairs={{0,16},{8,24},{16,0},{24,8},{32,48},{40,56},{48,32},{56,40},{64,80... | collective-permute-start | bytes 196616 | tf_op jit(solution)/shard_map/ppermute | solution.py:13
  567.6 8.8 %collective-permute-start.35 = (f32[128,128]{0,1:T(8,128)S(1)}, f32[128,128]{0,1:T(8,128)S(1)}, u32[]{:S(2)}, u32[]{:S(2)}) collective-permute-start(f32[128,128]{0,1:T(8,128)S(1)} %add.196), channel_id=1, source_target_pairs={{0,32},{8,40},{16,48},{24,56},{32,0},{40,8},{48,16},{56,24},{64,96... | collective-permute-start | bytes 196616 | tf_op jit(solution)/shard_map/ppermute | solution.py:13
  578.3 4.4 collective-permute-start.36
  582.7 6.0 collective-permute-start.37
  588.7 8.5 %collective-permute-start.38 = (f32[128,128]{0,1:T(8,128)S(1)}, f32[128,128]{0,1:T(8,128)S(1)}, u32[]{:S(2)}, u32[]{:S(2)}) collective-permute-start(f32[128,128]{0,1:T(8,128)S(1)} %add.199), channel_id=1, source_target_pairs={{0,32},{8,40},{16,48},{24,56},{32,0},{40,8},{48,16},{56,24},{64,96... | collective-permute-start | bytes 196616 | tf_op jit(solution)/shard_map/ppermute | solution.py:13
  597.1 4.4 collective-permute-start.39
  603.4 4.4 collective-permute-start.40
  607.8 6.0 collective-permute-start.41
  613.7 8.3 %collective-permute-start.42 = (f32[128,128]{0,1:T(8,128)S(1)}, f32[128,128]{0,1:T(8,128)S(1)}, u32[]{:S(2)}, u32[]{:S(2)}) collective-permute-start(f32[128,128]{0,1:T(8,128)S(1)} %add.203), channel_id=1, source_target_pairs={{0,32},{8,40},{16,48},{24,56},{32,0},{40,8},{48,16},{56,24},{64,96... | collective-permute-start | bytes 196616 | tf_op jit(solution)/shard_map/ppermute | solution.py:13
  622.0 4.4 collective-permute-start.43
  626.4 5.9 collective-permute-start.44
  (11 other events, 129.4 us)
Sparse Core Ops, SparseCore 0:
  109.7 139.7 all-reduce.2
  373.6 136.8 all-reduce.4
where the time goes:
time: 651 us; the launch traced here: 641 us
  waiting for transfers between devices  442 us (68%)
  starting transfers between devices  91.8 us (14%)
  matrix products  57.5 us (9%)
  blocking collectives  27.1 us (4%)
  between operations  14.4 us (2%)
  local copies, waits for them, and re-layouts  8.09 us (1%)
    psum x2, waiting for transfers between devices, body(): subtree_total = lax.psum(local_skel, 'leaf')  277 us
    ppermute x45, waiting for transfers between devices, partner(): lax.ppermute(x, axis, [(i, i ^ 1 << stride) for i in range(lax.axis_size(...  165 us
    ppermute x45, starting transfers between devices, partner(): lax.ppermute(x, axis, [(i, i ^ 1 << stride) for i in range(lax.axis_size(...  91.8 us
    dot_general x37, matrix products, matmul(): jnp.dot(left, right, precision=HI, preferred_element_type=jnp.float32)  31.4 us
    all_gather x2, blocking collectives, body(): every_skel = lax.all_gather(subtree_total[None], 'sub', axis=0, tiled=True)  27.1 us
    dot_general x17, matrix products, tmatmul(): lax.dot_general(left, right, (((0,), (0,)), ((), ())), precision=HI, pref...  22 us
  transfers between devices with their start and end apart: 47, of which 47 were waited for; matrix products, arithmetic and copies ran while one was open for 0% of the time, Pallas kernels for 0%

commit v1 on v0

v1 whole, which is shorter than its diff:
```python
import jax
import jax.numpy as jnp
from jax import lax
from jax.experimental import pallas as pl
from jax.experimental.pallas import tpu as pltpu
from jax.sharding import PartitionSpec as P

ROUNDS = 2
F32, BF16 = jnp.float32, jnp.bfloat16
M, K, R = 1024, 128, 128
NL = 5
NB = NL + 1
NZ, NY, NSUB = 8, 4, 8
BLK = R // NZ
MESH = pl.DeviceIdType.MESH
NN = (((1,), (0,)), ((), ()))
NT = (((1,), (1,)), ((), ()))
TN = (((0,), (0,)), ((), ()))


def split(x):
    hi = x.astype(BF16)
    return hi, (x - hi.astype(F32)).astype(BF16)


def dot(a, b, dims=NN):
    return lax.dot_general(a, b, dims, preferred_element_type=F32)


def dot3(a, b, dims=NN):
    (ah, al), (bh, bl) = a, b
    return dot(ah, bh, dims) + (dot(ah, bl, dims) + dot(al, bh, dims))


def cols(first, last=None):
    return slice(first * K, (first + 1 if last is None else last) * K)


SETUP_PAIRS = [(3, 2), (4, 2), (5, 2), (4, 3), (5, 3), (5, 4)]


def buffers():
    out = {
        "inv": pltpu.VMEM((M, M), BF16),
        "blk": pltpu.VMEM((M, M), BF16),
        "rhs": pltpu.VMEM((M, R), F32),
        "bas": pltpu.VMEM((NB, M, K), F32),
        "core": pltpu.VMEM((NL, K, K), F32),
        "coup": pltpu.VMEM((NSUB, K, K), F32),
        "bhi": pltpu.VMEM((M, NB * K), BF16),
        "blo": pltpu.VMEM((M, NB * K), BF16),
        "gram": pltpu.VMEM((NL, K, NB * K), F32),
        "chi": pltpu.VMEM((K, NSUB * K), BF16),
        "clo": pltpu.VMEM((K, NSUB * K), BF16),
        "xcat": pltpu.VMEM((M, 2 * R), BF16),
        "x": pltpu.VMEM((M, R), F32),
        "h10": pltpu.VMEM((2, K, K), F32),
        "loads": pltpu.SemaphoreType.DMA((8,)),
    }

    def ring(tag, n2, n3, n4):
        nm = n2 + n3 + n4
        out[tag + "rs_out"] = pltpu.VMEM((NZ, nm, BLK, K), F32)
        out[tag + "rs_in"] = pltpu.VMEM((NZ - 1, nm, BLK, K), F32)
        out[tag + "y_out"] = pltpu.VMEM((n3 + n4, BLK, K), F32)
        out[tag + "y_in"] = pltpu.VMEM((NY - 1, n3 + n4, BLK, K), F32)
        out[tag + "ag_near"] = pltpu.VMEM((NZ, n2, BLK, K), F32)
        out[tag + "ag_far"] = pltpu.VMEM((NZ, n3 + n4, BLK, K), F32)

    ring("setup_", 3, 2, 1)
    for k in range(ROUNDS + 1):
        ring(f"s{k}_", 1, 1, 2 if k < ROUNDS else 1)
        out[f"s{k}_quad_out"] = pltpu.VMEM((2, R, K), F32)
        out[f"s{k}_quad_in"] = pltpu.VMEM((3, R, K), F32)
        out[f"s{k}_pair_in"] = pltpu.VMEM((R, K), F32)
        if k < ROUNDS:
            out[f"s{k}_yall"] = pltpu.VMEM((NSUB, BLK, K), F32)
            out[f"s{k}_zall"] = pltpu.VMEM((NZ, BLK, K), F32)
    return out


NSEM = 160
SCRATCH = buffers()


def kernel(rhs_h, blk_h, inv_h, bas_h, core_h, skel_h, coup_h, out_ref, *scratch):
    names = list(SCRATCH)
    b = dict(zip(names, scratch[: len(names)]))
    send_sems, recv_sems = scratch[len(names) :]

    loads = [
        (bas_h, b["bas"].at[pl.ds(0, NL)]),
        (skel_h, b["bas"].at[NL]),
        (core_h, b["core"]),
        (rhs_h, b["rhs"]),
        (inv_h, b["inv"]),
        (coup_h, b["coup"]),
        (blk_h, b["blk"]),
    ]
    loads = [pltpu.make_async_copy(s, d, b["loads"].at[i]) for i, (s, d) in enumerate(loads)]
    for copy in loads:
        copy.start()
    l_bas, l_skel, l_core, l_rhs, l_inv, l_coup, l_blk = loads

    leaf, sub = lax.axis_index("leaf"), lax.axis_index("sub")
    y, z = lax.div(leaf, NZ), lax.rem(leaf, NZ)
    row = y * NZ
    quad = row + lax.div(z, 4) * 4
    z_peers = [row + lax.rem(z + NZ - d, NZ) for d in range(1, NZ)]
    quad_peers = [quad + lax.rem(z + 4 - d, 4) for d in range(1, 4)]
    pair_peer = leaf + 1 - 2 * lax.rem(z, 2)
    y_peers = [(y + 1 - 2 * lax.rem(y, 2)) * NZ + z, lax.rem(y + 2, NY) * NZ + z, (NY - 1 - y) * NZ + z]
    sub_peers = [lax.rem(sub + NSUB - d, NSUB) for d in range(1, NSUB)]

    barrier = pltpu.get_barrier_semaphore()
    for peer in z_peers + y_peers:
        pl.semaphore_signal(barrier, inc=1, device_id={"leaf": peer}, device_id_type=MESH)
    for peer in sub_peers:
        pl.semaphore_signal(barrier, inc=1, device_id={"sub": peer}, device_id_type=MESH)

    sent = []

    def send(src, dst, where):
        i = len(sent)
        copy = pltpu.make_async_remote_copy(
            src_ref=src,
            dst_ref=dst,
            send_sem=send_sems.at[i],
            recv_sem=recv_sems.at[i],
            device_id=where,
            device_id_type=MESH,
        )
        copy.start()
        sent.append(copy)
        return copy

    far_first = [3, 2, 4, 1, 5, 0, 6]

    def ring_start(tag, mats):
        out = b[tag + "rs_out"]
        for m, mat in enumerate(mats):
            out[:, m] = mat.reshape(NZ, BLK, K)
        return [
            send(out.at[lax.rem(z + NZ - d - 1, NZ)], b[tag + "rs_in"].at[d], {"leaf": z_peers[d]})
            for d in far_first
        ]

    def ring_reduce(tag, n2, n3, copies):
        for copy in copies:
            copy.wait_recv()
        total = b[tag + "rs_out"][z]
        for d in range(NZ - 1):
            total = total + b[tag + "rs_in"][d]
        b[tag + "y_out"][...] = total[n2:]
        y_copies = [
            send(b[tag + "y_out"].at[pl.ds(f, total.shape[0] - n2 - f)],
                 b[tag + "y_in"].at[e, pl.ds(f, total.shape[0] - n2 - f)], {"leaf": y_peers[e]})
            for e, f in ((1, n3), (2, n3), (0, 0))
        ]
        near = b[tag + "ag_near"]
        near[z] = total[:n2]
        near_copies = [send(near.at[z], near.at[z], {"leaf": z_peers[d]}) for d in far_first]
        return total[n2:], y_copies, near_copies

    def ring_far(tag, n3, total, y_copies):
        for copy in y_copies:
            copy.wait_recv()
        y_in = b[tag + "y_in"]
        third = total[:n3] + y_in[0, :n3]
        fourth = (total[n3:] + y_in[0, n3:]) + (y_in[1, n3:] + y_in[2, n3:])
        return third, fourth

    def gather(ref, block, axis_peers):
        ref[z] = block
        return [send(ref.at[z], ref.at[z], {"leaf": z_peers[d]}) for d in far_first]

    def wait(copies):
        for copy in copies:
            copy.wait_recv()

    bhi, blo, gram = b["bhi"], b["blo"], b["gram"]

    l_bas.wait()
    l_skel.wait()
    for l in range(NB):
        bhi[:, cols(l)], blo[:, cols(l)] = split(b["bas"][l])
    for j in range(NL):
        right = slice((j + 1) * K, NB * K)
        here_hi, here_lo = bhi[:, cols(j)], blo[:, cols(j)]
        gram[j, :, right] = dot(here_hi, bhi[:, right], TN) + (
            dot(here_hi, blo[:, right], TN) + dot(here_lo, bhi[:, right], TN)
        )
    l_core.wait()
    core = [split(b["core"][l]) for l in range(NL)]

    def coupled(l, j):
        return dot3(core[j], split(gram[j, :, cols(l)]), TN)

    pl.semaphore_wait(barrier, len(z_peers) + len(y_peers) + len(sub_peers))
    b["h10"][0] = coupled(1, 0)
    h10_copy = send(b["h10"].at[0], b["h10"].at[1], {"leaf": pair_peer})
    setup_rs = ring_start("setup_", [coupled(l, j) for l, j in SETUP_PAIRS])

    l_coup.wait()
    for t in range(NSUB):
        b["chi"][:, cols(t)], b["clo"][:, cols(t)] = split(b["coup"][t])

    def spread(value):
        b["xcat"][:, :R], b["xcat"][:, R:] = split(value)

    def leaf_product(mat, finish):
        @pl.loop(0, M // 256)
        def _(t):
            rows = pl.ds(pl.multiple_of(t * 256, 256), 256)
            both = dot(mat[rows, :], b["xcat"][...])
            finish(rows, both[:, :R] + both[:, R:])

    def put_x(rows, value):
        b["x"][rows, :] = value

    def project():
        hi, lo = split(b["x"][...].T)
        both = dot(jnp.concatenate([hi, lo], axis=0), bhi[...])
        return both[:R] + both[R:] + dot(hi, blo[...])

    def expand(first, last, moved):
        hi, lo = split(moved)
        bh, bl = bhi[:, cols(first, last)], blo[:, cols(first, last)]
        both = dot(bh, jnp.concatenate([hi, lo], axis=0), NT)
        return both[:, :R] + both[:, R:] + dot(bl, hi, NT)

    h = {}
    l_rhs.wait()
    l_inv.wait()
    res = b["rhs"]
    for k in range(ROUNDS + 1):
        tag = f"s{k}_"
        last = k == ROUNDS
        spread(res[...])
        leaf_product(b["inv"], put_x)
        q = project()
        if k == 0:
            wait([h10_copy])
            h[1, 0] = split(b["h10"][0] + b["h10"][1])

        u0 = q[:, cols(0)]
        u1 = q[:, cols(1)] - dot3(split(u0), h[1, 0])
        out = b[tag + "quad_out"]
        out[1] = u1
        out[0] = u0
        near = [send(out.at[1], b[tag + "quad_in"].at[d], {"leaf": quad_peers[d]}) for d in (1, 2, 0)]
        near.append(send(out.at[0], b[tag + "pair_in"], {"leaf": pair_peer}))

        if k == 0:
            total, y_copies, near_copies = ring_reduce("setup_", 3, 2, setup_rs)
            third, fourth = ring_far("setup_", 2, total, y_copies)
            far_copies = gather(b["setup_ag_far"], jnp.concatenate([third, fourth], axis=0), None)

        wait(near)
        quad_in = b[tag + "quad_in"]
        g0 = u0 + b[tag + "pair_in"][...]
        g1 = (u1 + quad_in[0]) + (quad_in[1] + quad_in[2])
        m01 = jnp.concatenate([dot3(split(g0), core[0], NT), dot3(split(g1), core[1], NT)], axis=1)
        nb = NL if last else NB
        right = slice(2 * K, nb * K)
        both = jnp.concatenate([gram[0, :, right], gram[1, :, right]], axis=0)
        p = q[:, right] - dot3(split(m01), split(both))

        if k == 0:
            wait(near_copies)
            for i in range(3):
                h[SETUP_PAIRS[i]] = split(b["setup_ag_near"][:, i].reshape(K, K))
            wait(far_copies)
            for i in range(3):
                h[SETUP_PAIRS[3 + i]] = split(b["setup_ag_far"][:, i].reshape(K, K))

        u = []
        for l in range(2, nb):
            ul = p[:, cols(l - 2)]
            for j in range(2, l):
                ul = ul - dot3(u[j - 2][1], h[l, j])
            u.append((ul, split(ul)))
        rs = ring_start(tag, [ul for ul, _ in u])
        b["x"][...] -= expand(0, 2, m01)
        total, y_copies, near_copies = ring_reduce(tag, 1, 1, rs)
        third, fourth = ring_far(tag, 1, total, y_copies)
        if last:
            far = jnp.concatenate([third, fourth], axis=0)
        else:
            far = jnp.concatenate([third, fourth], axis=0)
            yall = b[tag + "yall"]
            yall[sub] = fourth[1]
            sub_copies = [send(yall.at[sub], yall.at[sub], {"sub": peer}) for peer in sub_peers]
            far = far[:2]
        ag_far = b[tag + "ag_far"]
        ag_far[z, :2] = far
        far_copies = [send(ag_far.at[z, pl.ds(0, 2)], ag_far.at[z, pl.ds(0, 2)], {"leaf": z_peers[d]}) for d in far_first]
        if not last:
            wait(sub_copies)
            hi, lo = split(jnp.concatenate([yall[t] for t in range(NSUB)], axis=1))
            both = dot(jnp.concatenate([hi, lo], axis=0), b["chi"][...], NT)
            zall = b[tag + "zall"]
            z_copies = gather(zall, both[:BLK] + both[BLK:] + dot(hi, b["clo"][...], NT), None)
        wait(near_copies)
        wait(far_copies)
        g2 = b[tag + "ag_near"][:, 0].reshape(R, K)
        g3 = ag_far[:, 0].reshape(R, K)
        g4 = ag_far[:, 1].reshape(R, K)
        moved = jnp.concatenate(
            [dot3(split(g), core[l], NT) for l, g in ((2, g2), (3, g3), (4, g4))], axis=1
        )
        dx = b["x"][...] - expand(2, NL, moved)
        if k == 0:
            out_ref[...] = dx
        else:
            out_ref[...] += dx
        if not last:
            if k == 0:
                l_blk.wait()
            spread(dx)

            def take(rows, value):
                res[rows, :] -= value

            leaf_product(b["blk"], take)
            wait(z_copies)
            res[...] -= expand(NL, NB, zall[...].reshape(R, K))

    for copy in sent:
        copy.wait_send()


def body(rhs, leaf_block, leaf_inverse, level_basis, level_core, skeleton_basis, coupling):
    hbm = pl.BlockSpec(memory_space=pl.ANY)
    out = pl.pallas_call(
        kernel,
        out_shape=jax.ShapeDtypeStruct((M, R), F32),
        in_specs=[hbm] * 7,
        out_specs=pl.BlockSpec(memory_space=pltpu.VMEM),
        scratch_shapes=[
            *SCRATCH.values(),
            pltpu.SemaphoreType.DMA((NSEM,)),
            pltpu.SemaphoreType.DMA((NSEM,)),
        ],
        compiler_params=pltpu.CompilerParams(
            collective_id=0, has_side_effects=True, vmem_limit_bytes=56 * 2**20
        ),
        cost_estimate=pl.CostEstimate(flops=8 * 10**9, bytes_accessed=10 * 10**6, transcendentals=0),
        name="ridge_rounds",
    )(
        rhs[0, 0],
        leaf_block[0, 0],
        leaf_inverse[0, 0],
        level_basis[0, 0],
        level_core[0, 0],
        skeleton_basis[0, 0],
        coupling[0],
    )
    return out[None, None]


def solution(mesh):
    return jax.shard_map(
        body,
        mesh=mesh,
        in_specs=(
            P("sub", "leaf", None, None),
            P("sub", "leaf", None, None),
            P("sub", "leaf", None, None),
            P("sub", "leaf", None, None, None),
            P("sub", "leaf", None, None, None),
            P("sub", "leaf", None, None),
            P("sub", None, None, None),
        ),
        out_specs=P("sub", "leaf", None, None),
        check_vma=False,
    )
```

time: 651 us -> 117 us (0.18); the launches traced: 641 us -> 117 us
  waiting for transfers between devices: 442 us -> 0 us
  Pallas kernels: 0 us -> 115 us
  starting transfers between devices: 91.8 us -> 0 us
  matrix products: 57.5 us -> 0 us
  blocking collectives: 27.1 us -> 0 us
  between operations: 14.4 us -> 0.01 us
    psum x2 -> x0, waiting for transfers between devices: 277 us -> none  [body(): subtree_total = lax.psum(local_skel, 'leaf')]
    ppermute x45 -> x0, waiting for transfers between devices: 165 us -> none  [partner(): lax.ppermute(x, axis, [(i, i ^ 1 << stride) for i in range(lax.axis_size(...]
    pallas_call x0 -> x1, Pallas kernels: none -> 115 us  [body(): pl.pallas_call(kernel, out_shape=jax.ShapeDtypeStruct((M, R), F32), in_sp...]
    ppermute x45 -> x0, starting transfers between devices: 91.8 us -> none  [partner(): lax.ppermute(x, axis, [(i, i ^ 1 << stride) for i in range(lax.axis_size(...]
    dot_general x56 -> x0, matrix products: 57.5 us -> none  [the longest x37 31.4 us: matmul(): jnp.dot(left, right, precision=HI, preferred_element_type=jnp.float32)]
    all_gather x2 -> x0, blocking collectives: 27.1 us -> none  [body(): every_skel = lax.all_gather(subtree_total[None], 'sub', axis=0, tiled=True)]
  transfers between devices with their start and end apart: 47 -> 0, of which waited for: 47 -> 0; matrix products, arithmetic and copies ran while one was open for 0% -> 0% of each run, Pallas kernels for 0% -> 0%
where the time goes in v1:
time: 117 us
  Pallas kernels  115 us (98%)
  local copies, waits for them, and re-layouts  1.87 us (2%)
    pallas_call x1, Pallas kernels, body(): pl.pallas_call(kernel, out_shape=jax.ShapeDtypeStruct((M, R), F32), in_sp...  115 us

profile of v1, /device:TPU:6, one launch (start us, length us, event | category | flops | bytes accessed | tf_op | source)
XLA Modules:
  0.0 116.6 jit_solution(5946913920159225857)
XLA Ops:
  0.0 114.8 %ridge_rounds.1 = f32[1024,128]{1,0:T(8,128)} custom-call(f32[1024,128]{1,0:T(8,128)} %bitcast.12, bf16[1024,1024]{1,0:T(8,128)(2,1)} %bitcast.10, bf16[1024,1024]{1,0:T(8,128)(2,1)} %bitcast.11, f32[5,1024,128]{2,1,0:T(8,128)} %bitcast.9, f32[5,128,128]{2,1,0:T(8,128)} %bitcast.15, f32[1024,128]{1,0:T(8,128)} %bitcast.13, f32[8,128,128]{2,1,0:T(8,128)} %bitcast.14), custom_call_target="tpu_custom_call" | custom-call | flops 8000000000 | bytes 10000000 | tf_op jit(solution)/shard_map/ridge_rounds/pallas_call | solution.py:335
  114.8 1.9 %copy.9 = f32[1,1,1024,128]{3,2,1,0:T(8,128)} copy(f32[1,1,1024,128]{3,2,1,0:T(8,128)} %bitcast.8) | data formatting | bytes 1048576

commit v2 on v1

v2 whole, which is shorter than its diff:
```python
import jax
import jax.numpy as jnp
from jax import lax
from jax.experimental import pallas as pl
from jax.experimental.pallas import tpu as pltpu
from jax.sharding import PartitionSpec as P

ROUNDS = 2
F32, BF16 = jnp.float32, jnp.bfloat16
M, K, R = 1024, 128, 128
NL = 5
NB = NL + 1
NF = NL - 2 + 1
NZ, NY, NSUB = 8, 4, 8
BLK = R // NZ
MESH = pl.DeviceIdType.MESH
NN = (((1,), (0,)), ((), ()))
NT = (((1,), (1,)), ((), ()))
TN = (((0,), (0,)), ((), ()))


def split(x):
    hi = x.astype(BF16)
    return hi, (x - hi.astype(F32)).astype(BF16)


def dot(a, b, dims=NN):
    return lax.dot_general(a, b, dims, preferred_element_type=F32)


def dot3(a, b, dims=NN):
    (ah, al), (bh, bl) = a, b
    return dot(ah, bh, dims) + (dot(ah, bl, dims) + dot(al, bh, dims))


def cols(first, last=None):
    return slice(first * K, (first + 1 if last is None else last) * K)


def buffers():
    out = {
        "inv": pltpu.VMEM((M, M), BF16),
        "blk": pltpu.VMEM((M, M), BF16),
        "res": pltpu.VMEM((M, R), F32),
        "bas": pltpu.VMEM((NB, M, K), F32),
        "core": pltpu.VMEM((NL, K, K), F32),
        "coup": pltpu.VMEM((NSUB, K, K), F32),
        "bhi": pltpu.VMEM((M, NB * K), BF16),
        "blo": pltpu.VMEM((M, NB * K), BF16),
        "dhi": pltpu.VMEM((M, NF * K), BF16),
        "dlo": pltpu.VMEM((M, NF * K), BF16),
        "vhi": pltpu.VMEM((M, NF * K), BF16),
        "vlo": pltpu.VMEM((M, NF * K), BF16),
        "ehi": pltpu.VMEM((NF * K, NB * K), BF16),
        "elo": pltpu.VMEM((NF * K, NB * K), BF16),
        "gram": pltpu.VMEM((NL, K, NB * K), F32),
        "chi": pltpu.VMEM((K, NSUB * K), BF16),
        "clo": pltpu.VMEM((K, NSUB * K), BF16),
        "xcat": pltpu.VMEM((M, 2 * R), BF16),
        "x": pltpu.VMEM((M, R), F32),
        "x1": pltpu.VMEM((M, R), F32),
        "h10": pltpu.VMEM((2, K, K), F32),
        "loads": pltpu.SemaphoreType.DMA((NB + 5,)),
    }

    def ring(tag, near, far, reduced=True):
        out[tag + "rs_out"] = pltpu.VMEM((NZ, near + far, BLK, K), F32)
        out[tag + "rs_in"] = pltpu.VMEM((NZ - 1, near + far, BLK, K), F32)
        if far:
            out[tag + "y_out"] = pltpu.VMEM((far, BLK, K), F32)
            out[tag + "y_in"] = pltpu.VMEM((NY - 1, far, BLK, K), F32)
        if near:
            out[tag + "near"] = pltpu.VMEM((NZ, near, BLK, K), F32)
        if far and reduced:
            out[tag + "far"] = pltpu.VMEM((NZ, min(far, 2), BLK, K), F32)

    ring("h1_", 2, 1)
    ring("h2_", 1, 2)
    ring("s0y_", 0, 1, False)
    for k in range(ROUNDS + 1):
        ring(f"s{k}n_", 1, 0)
        ring(f"s{k}f_", 0, 3 if k == 1 else 2)
        out[f"s{k}_quad_out"] = pltpu.VMEM((2, R, K), F32)
        out[f"s{k}_quad_in"] = pltpu.VMEM((3, R, K), F32)
        out[f"s{k}_pair_in"] = pltpu.VMEM((R, K), F32)
        if k < ROUNDS:
            out[f"s{k}_yall"] = pltpu.VMEM((NSUB, BLK, K), F32)
            out[f"s{k}_zall"] = pltpu.VMEM((NZ, 1, BLK, K), F32)
    return out


NSEM = 200
SCRATCH = buffers()


def kernel(rhs_h, blk_h, inv_h, bas_h, core_h, skel_h, coup_h, out_ref, *scratch):
    names = list(SCRATCH)
    b = dict(zip(names, scratch[: len(names)]))
    send_sems, recv_sems = scratch[len(names) :]

    loads = [(bas_h.at[l], b["bas"].at[l]) for l in range(NL)] + [
        (skel_h, b["bas"].at[NL]),
        (core_h, b["core"]),
        (rhs_h, b["res"]),
        (inv_h, b["inv"]),
        (blk_h, b["blk"]),
        (coup_h, b["coup"]),
    ]
    loads = [pltpu.make_async_copy(s, d, b["loads"].at[i]) for i, (s, d) in enumerate(loads)]
    for copy in loads[: NB + 1]:
        copy.start()
    l_core, l_rhs, l_inv, l_blk, l_coup = loads[NB:]

    leaf, sub = lax.axis_index("leaf"), lax.axis_index("sub")
    y, z = lax.div(leaf, NZ), lax.rem(leaf, NZ)
    row = y * NZ
    quad = row + lax.div(z, 4) * 4
    z_peers = [row + lax.rem(z + NZ - d, NZ) for d in range(1, NZ)]
    quad_peers = [quad + lax.rem(z + 4 - d, 4) for d in range(1, 4)]
    pair_peer = leaf + 1 - 2 * lax.rem(z, 2)
    y_peers = [(y + 1 - 2 * lax.rem(y, 2)) * NZ + z, lax.rem(y + 2, NY) * NZ + z, (NY - 1 - y) * NZ + z]
    sub_peers = [lax.rem(sub + NSUB - d, NSUB) for d in range(1, NSUB)]

    barrier = pltpu.get_barrier_semaphore()
    for peer in z_peers + y_peers:
        pl.semaphore_signal(barrier, inc=1, device_id={"leaf": peer}, device_id_type=MESH)
    for peer in sub_peers:
        pl.semaphore_signal(barrier, inc=1, device_id={"sub": peer}, device_id_type=MESH)

    sent = []

    def send(src, dst, where):
        i = len(sent)
        copy = pltpu.make_async_remote_copy(
            src_ref=src,
            dst_ref=dst,
            send_sem=send_sems.at[i],
            recv_sem=recv_sems.at[i],
            device_id=where,
            device_id_type=MESH,
        )
        copy.start()
        sent.append(copy)
        return copy

    def wait(copies):
        for copy in copies:
            copy.wait_recv()

    far_first = [3, 2, 4, 1, 5, 0, 6]

    def rs_start(tag, mats):
        out = b[tag + "rs_out"]
        for m, mat in enumerate(mats):
            out[:, m] = mat.reshape(NZ, BLK, K)
        return [
            send(out.at[lax.rem(z + NZ - d - 1, NZ)], b[tag + "rs_in"].at[d], {"leaf": z_peers[d]})
            for d in far_first
        ]

    def rs_finish(tag, copies):
        wait(copies)
        total = b[tag + "rs_out"][z]
        for d in range(NZ - 1):
            total = total + b[tag + "rs_in"][d]
        return total

    def y_start(tag, total, two):
        n = total.shape[0]
        y_out, y_in = b[tag + "y_out"], b[tag + "y_in"]
        y_out[...] = total
        return [
            send(y_out.at[pl.ds(f, n - f)], y_in.at[e, pl.ds(f, n - f)], {"leaf": y_peers[e]})
            for e, f in ((1, two), (2, two), (0, 0))
            if n > f
        ]

    def y_finish(tag, total, two, copies):
        wait(copies)
        y_in = b[tag + "y_in"]
        parts = [total[i] + y_in[0, i] for i in range(two)]
        parts += [(total[i] + y_in[0, i]) + (y_in[1, i] + y_in[2, i]) for i in range(two, total.shape[0])]
        return parts

    def ag_start(name, blocks):
        ref = b[name]
        for i, block in enumerate(blocks):
            ref[z, i] = block
        return [send(ref.at[z], ref.at[z], {"leaf": z_peers[d]}) for d in far_first]

    def ag_finish(name, copies):
        wait(copies)
        return [b[name][:, i].reshape(R, K) for i in range(b[name].shape[1])]

    bhi, blo, gram = b["bhi"], b["blo"], b["gram"]

    for l in range(NB):
        loads[l].wait()
        bhi[:, cols(l)], blo[:, cols(l)] = split(b["bas"][l])
    l_inv.start()
    l_rhs.start()
    for j in range(NL):
        right = slice((j + 1) * K, NB * K)
        here_hi, here_lo = bhi[:, cols(j)], blo[:, cols(j)]
        gram[j, :, right] = dot(here_hi, bhi[:, right], TN) + (
            dot(here_hi, blo[:, right], TN) + dot(here_lo, bhi[:, right], TN)
        )
    l_blk.start()
    l_coup.start()
    l_core.wait()
    core = [split(b["core"][l]) for l in range(NL)]

    def coupled(l, j):
        return dot3(core[j], split(gram[j, :, cols(l)]), TN)

    b["h10"][0] = coupled(1, 0)
    h1_mats = [coupled(3, 2), coupled(4, 2), coupled(4, 3)]
    pl.semaphore_wait(barrier, len(z_peers) + len(y_peers) + len(sub_peers))
    h10_copy = send(b["h10"].at[0], b["h10"].at[1], {"leaf": pair_peer})
    h1_rs = rs_start("h1_", h1_mats)

    def spread(value):
        b["xcat"][:, :R], b["xcat"][:, R:] = split(value)

    def leaf_product(mat, finish):
        @pl.loop(0, M // 256)
        def _(t):
            rows = pl.ds(pl.multiple_of(t * 256, 256), 256)
            both = dot(mat[rows, :], b["xcat"][...])
            finish(rows, both[:, :R] + both[:, R:])

    def put_x(rows, value):
        b["x"][rows, :] = value

    def reduce_res(rows, value):
        b["res"][rows, :] -= value

    def project():
        hi, lo = split(b["x"][...].T)
        both = dot(jnp.concatenate([hi, lo], axis=0), bhi[...])
        return both[:R] + both[R:] + dot(hi, blo[...])

    def expand(high, low, where, moved):
        hi, lo = split(moved)
        both = dot(high[:, where], jnp.concatenate([hi, lo], axis=0), NT)
        return both[:, :R] + both[:, R:] + dot(low[:, where], hi, NT)

    def composed(where, moved):
        hi, lo = split(moved)
        both = dot(jnp.concatenate([hi, lo], axis=0), b["ehi"][where, :])
        return both[:R] + both[R:] + dot(hi, b["elo"][where, :])

    def block_bases():
        @pl.loop(0, M // 256)
        def _(t):
            rows = pl.ds(pl.multiple_of(t * 256, 256), 256)
            some = cols(2, NL)
            value = dot(b["blk"][rows, :], bhi[:, some]) + dot(b["blk"][rows, :], blo[:, some])
            b["dhi"][rows, cols(0, NF - 1)], b["dlo"][rows, cols(0, NF - 1)] = split(value)

        b["dhi"][:, cols(NF - 1)] = bhi[:, cols(NL)]
        b["dlo"][:, cols(NF - 1)] = blo[:, cols(NL)]

    def inverse_bases(first, last):
        @pl.loop(first, last)
        def _(t):
            rows = pl.ds(pl.multiple_of(t * 256, 256), 256)
            value = dot(b["inv"][rows, :], b["dhi"][...]) + dot(b["inv"][rows, :], b["dlo"][...])
            b["vhi"][rows, :], b["vlo"][rows, :] = split(value)

    def project_bases(first, last):
        for c in range(first, last):
            hi, lo = b["vhi"][:, cols(c)], b["vlo"][:, cols(c)]
            value = dot(hi, bhi[...], TN) + (dot(hi, blo[...], TN) + dot(lo, bhi[...], TN))
            b["ehi"][cols(c), :], b["elo"][cols(c), :] = split(value)

    h = {}

    def level_start(k, q):
        u0 = q[:, cols(0)]
        u1 = q[:, cols(1)] - dot3(split(u0), h[1, 0])
        out = b[f"s{k}_quad_out"]
        out[1] = u1
        out[0] = u0
        copies = [
            send(out.at[1], b[f"s{k}_quad_in"].at[d], {"leaf": quad_peers[d]}) for d in (1, 2, 0)
        ]
        return u0, u1, copies + [send(out.at[0], b[f"s{k}_pair_in"], {"leaf": pair_peer})]

    def level_finish(k, q, nb, started):
        u0, u1, copies = started
        wait(copies)
        quad_in = b[f"s{k}_quad_in"]
        g0 = u0 + b[f"s{k}_pair_in"][...]
        g1 = (u1 + quad_in[0]) + (quad_in[1] + quad_in[2])
        m01 = jnp.concatenate([dot3(split(g0), core[0], NT), dot3(split(g1), core[1], NT)], axis=1)
        right = slice(2 * K, nb * K)
        both = jnp.concatenate([gram[0, :, right], gram[1, :, right]], axis=0)
        return m01, q[:, right] - dot3(split(m01), split(both))

    def corrected(p, l, u):
        ul = p[:, cols(l - 2)]
        for j in range(2, l):
            ul = ul - dot3(u[j], h[l, j])
        u[l] = split(ul)
        return ul

    def partial(m01):
        x1 = b["x"][...] - expand(bhi, blo, cols(0, 2), m01)
        b["x1"][...] = x1
        spread(x1)
        leaf_product(b["blk"], reduce_res)
        spread(b["res"][...])
        leaf_product(b["inv"], put_x)
        return project()

    def moved_of(near, far):
        return jnp.concatenate(
            [dot3(split(g), core[l], NT) for l, g in zip((2, 3, 4), (near[0], far[0], far[1]))], axis=1
        )

    def sub_start(k, block):
        yall = b[f"s{k}_yall"]
        yall[sub] = block
        return [send(yall.at[sub], yall.at[sub], {"sub": peer}) for peer in sub_peers]

    def sub_finish(k, copies):
        wait(copies)
        yall = b[f"s{k}_yall"]
        hi, lo = split(jnp.concatenate([yall[t] for t in range(NSUB)], axis=1))
        both = dot(jnp.concatenate([hi, lo], axis=0), b["chi"][...], NT)
        return ag_start(f"s{k}_zall", [both[:BLK] + both[BLK:] + dot(hi, b["clo"][...], NT)])

    def carry(moved, mixed):
        all_moved = jnp.concatenate([moved, -mixed], axis=1)
        b["x"][...] += expand(b["vhi"], b["vlo"], cols(0, NF), all_moved)
        b["res"][...] += expand(b["dhi"], b["dlo"], cols(0, NF), all_moved)

    l_rhs.wait()
    l_inv.wait()
    spread(b["res"][...])
    leaf_product(b["inv"], put_x)
    q = project()
    wait([h10_copy])
    h[1, 0] = split(b["h10"][0] + b["h10"][1])
    started = level_start(0, q)
    h2_rs = rs_start("h2_", [coupled(5, 2), coupled(5, 3), coupled(5, 4)])
    l_blk.wait()
    block_bases()
    l_coup.wait()
    for t in range(NSUB):
        b["chi"][:, cols(t)], b["clo"][:, cols(t)] = split(b["coup"][t])
    total = rs_finish("h1_", h1_rs)
    h1_total = total[2:]
    h1_y = y_start("h1_", h1_total, 1)
    h1_near = ag_start("h1_near", [total[0], total[1]])
    inverse_bases(0, 2)
    h1_far = ag_start("h1_far", y_finish("h1_", h1_total, 1, h1_y))
    total = rs_finish("h2_", h2_rs)
    h2_total = total[1:]
    h2_y = y_start("h2_", h2_total, 1)
    h2_near = ag_start("h2_near", [total[0]])
    inverse_bases(2, 4)
    m01, p = level_finish(0, q, NB, started)
    h2_far = ag_start("h2_far", y_finish("h2_", h2_total, 1, h2_y))
    h[3, 2], h[4, 2] = (split(a) for a in ag_finish("h1_near", h1_near))
    (h[4, 3],) = (split(a) for a in ag_finish("h1_far", h1_far))
    u = {}
    near_rs = rs_start("s0n_", [corrected(p, 2, u)])
    far_rs = rs_start("s0f_", [corrected(p, 3, u), corrected(p, 4, u)])
    q = partial(m01)
    (h[5, 2],) = (split(a) for a in ag_finish("h2_near", h2_near))
    h[5, 3], h[5, 4] = (split(a) for a in ag_finish("h2_far", h2_far))
    skel_rs = rs_start("s0y_", [corrected(p, 5, u)])
    far_total = rs_finish("s0f_", far_rs)
    far_y = y_start("s0f_", far_total, 1)
    near_ag = ag_start("s0n_near", [rs_finish("s0n_", near_rs)[0]])
    project_bases(0, 2)
    far_ag = ag_start("s0f_far", y_finish("s0f_", far_total, 1, far_y))
    skel_total = rs_finish("s0y_", skel_rs)
    skel_y = y_start("s0y_", skel_total, 0)
    project_bases(2, 4)
    sub_copies = sub_start(0, y_finish("s0y_", skel_total, 0, skel_y)[0])
    moved = moved_of(ag_finish("s0n_near", near_ag), ag_finish("s0f_far", far_ag))
    q = q + composed(cols(0, NF - 1), moved)
    mixed_copies = sub_finish(0, sub_copies)
    out_ref[...] = b["x1"][...] - expand(bhi, blo, cols(2, NL), moved)

    (mixed,) = ag_finish("s0_zall", mixed_copies)
    q = q - composed(cols(NF - 1), mixed)
    started = level_start(1, q)
    carry(moved, mixed)
    m01, p = level_finish(1, q, NB, started)
    u = {}
    near_rs = rs_start("s1n_", [corrected(p, 2, u)])
    far_rs = rs_start("s1f_", [corrected(p, l, u) for l in (3, 4, 5)])
    q = partial(m01)
    far_total = rs_finish("s1f_", far_rs)
    far_y = y_start("s1f_", far_total, 1)
    near_ag = ag_start("s1n_near", [rs_finish("s1n_", near_rs)[0]])
    far = y_finish("s1f_", far_total, 1, far_y)
    sub_copies = sub_start(1, far[2])
    far_ag = ag_start("s1f_far", far[:2])
    mixed_copies = sub_finish(1, sub_copies)
    moved = moved_of(ag_finish("s1n_near", near_ag), ag_finish("s1f_far", far_ag))
    q = q + composed(cols(0, NF - 1), moved)
    out_ref[...] += b["x1"][...] - expand(bhi, blo, cols(2, NL), moved)

    (mixed,) = ag_finish("s1_zall", mixed_copies)
    q = q - composed(cols(NF - 1), mixed)
    started = level_start(2, q)
    all_moved = jnp.concatenate([moved, -mixed], axis=1)
    b["x"][...] += expand(b["vhi"], b["vlo"], cols(0, NF), all_moved)
    m01, p = level_finish(2, q, NL, started)
    u = {}
    near_rs = rs_start("s2n_", [corrected(p, 2, u)])
    far_rs = rs_start("s2f_", [corrected(p, l, u) for l in (3, 4)])
    out_ref[...] += b["x"][...] - expand(bhi, blo, cols(0, 2), m01)
    far_total = rs_finish("s2f_", far_rs)
    far_y = y_start("s2f_", far_total, 1)
    near_ag = ag_start("s2n_near", [rs_finish("s2n_", near_rs)[0]])
    far_ag = ag_start("s2f_far", y_finish("s2f_", far_total, 1, far_y))
    moved = moved_of(ag_finish("s2n_near", near_ag), ag_finish("s2f_far", far_ag))
    out_ref[...] -= expand(bhi, blo, cols(2, NL), moved)

    for copy in sent:
        copy.wait_send()


def body(rhs, leaf_block, leaf_inverse, level_basis, level_core, skeleton_basis, coupling):
    hbm = pl.BlockSpec(memory_space=pl.ANY)
    out = pl.pallas_call(
        kernel,
        out_shape=jax.ShapeDtypeStruct((M, R), F32),
        in_specs=[hbm] * 7,
        out_specs=pl.BlockSpec(memory_space=pltpu.VMEM),
        scratch_shapes=[
            *SCRATCH.values(),
            pltpu.SemaphoreType.DMA((NSEM,)),
            pltpu.SemaphoreType.DMA((NSEM,)),
        ],
        compiler_params=pltpu.CompilerParams(
            collective_id=0, has_side_effects=True, vmem_limit_bytes=56 * 2**20
        ),
        cost_estimate=pl.CostEstimate(flops=8 * 10**9, bytes_accessed=10 * 10**6, transcendentals=0),
        name="ridge_rounds",
    )(
        rhs[0, 0],
        leaf_block[0, 0],
        leaf_inverse[0, 0],
        level_basis[0, 0],
        level_core[0, 0],
        skeleton_basis[0, 0],
        coupling[0],
    )
    return out[None, None]


def solution(mesh):
    return jax.shard_map(
        body,
        mesh=mesh,
        in_specs=(
            P("sub", "leaf", None, None),
            P("sub", "leaf", None, None),
            P("sub", "leaf", None, None),
            P("sub", "leaf", None, None, None),
            P("sub", "leaf", None, None, None),
            P("sub", "leaf", None, None),
            P("sub", None, None, None),
        ),
        out_specs=P("sub", "leaf", None, None),
        check_vma=False,
    )
```

time: 117 us -> 113 us (0.966)
  Pallas kernels: 115 us -> 111 us
    pallas_call x1, Pallas kernels: 115 us -> 111 us  [body(): pl.pallas_call(kernel, out_shape=jax.ShapeDtypeStruct((M, R), F32), in_sp...]
where the time goes in v2:
time: 113 us
  Pallas kernels  111 us (98%)
  local copies, waits for them, and re-layouts  1.87 us (2%)
    pallas_call x1, Pallas kernels, body(): pl.pallas_call(kernel, out_shape=jax.ShapeDtypeStruct((M, R), F32), in_sp...  111 us

profile of v2, /device:TPU:6, one launch (start us, length us, event | category | flops | bytes accessed | tf_op | source)
XLA Modules:
  0.0 113.3 jit_solution(8836124636421873968)
XLA Ops:
  0.0 111.4 %ridge_rounds.1 = f32[1024,128]{1,0:T(8,128)} custom-call(f32[1024,128]{1,0:T(8,128)} %bitcast.12, bf16[1024,1024]{1,0:T(8,128)(2,1)} %bitcast.10, bf16[1024,1024]{1,0:T(8,128)(2,1)} %bitcast.11, f32[5,1024,128]{2,1,0:T(8,128)} %bitcast.9, f32[5,128,128]{2,1,0:T(8,128)} %bitcast.15, f32[1024,128]{1,0:T(8,128)} %bitcast.13, f32[8,128,128]{2,1,0:T(8,128)} %bitcast.14), custom_call_target="tpu_custom_call" | custom-call | flops 8000000000 | bytes 10000000 | tf_op jit(solution)/shard_map/ridge_rounds/pallas_call | solution.py:432
  111.5 1.9 %copy.9 = f32[1,1,1024,128]{3,2,1,0:T(8,128)} copy(f32[1,1,1024,128]{3,2,1,0:T(8,128)} %bitcast.8) | data formatting | bytes 1048576

commit v3 on v2

--- a/solution.py
+++ b/solution.py
@@ -12,7 +12,8 @@
 NB = NL + 1
 NF = NL - 2 + 1
 NZ, NY, NSUB = 8, 4, 8
-BLK = R // NZ
+NH = 1
+RH = R // NH
 MESH = pl.DeviceIdType.MESH
 NN = (((1,), (0,)), ((), ()))
 NT = (((1,), (1,)), ((), ()))
@@ -63,33 +64,30 @@
         "loads": pltpu.SemaphoreType.DMA((NB + 5,)),
     }
 
-    def ring(tag, near, far, reduced=True):
-        out[tag + "rs_out"] = pltpu.VMEM((NZ, near + far, BLK, K), F32)
-        out[tag + "rs_in"] = pltpu.VMEM((NZ - 1, near + far, BLK, K), F32)
+    def ring(tag, near, far, back, blk):
+        out[tag + "rs_out"] = pltpu.VMEM((NZ, near + far, blk, K), F32)
+        out[tag + "rs_in"] = pltpu.VMEM((NZ - 1, near + far, blk, K), F32)
         if far:
-            out[tag + "y_out"] = pltpu.VMEM((far, BLK, K), F32)
-            out[tag + "y_in"] = pltpu.VMEM((NY - 1, far, BLK, K), F32)
-        if near:
-            out[tag + "near"] = pltpu.VMEM((NZ, near, BLK, K), F32)
-        if far and reduced:
-            out[tag + "far"] = pltpu.VMEM((NZ, min(far, 2), BLK, K), F32)
-
-    ring("h1_", 2, 1)
-    ring("h2_", 1, 2)
-    ring("s0y_", 0, 1, False)
+            out[tag + "y_out"] = pltpu.VMEM((far, blk, K), F32)
+            out[tag + "y_in"] = pltpu.VMEM((NY - 1, far, blk, K), F32)
+        out[tag + "ag"] = pltpu.VMEM((NZ, near + back, blk, K), F32)
+
+    ring("hf_", 0, 3, 3, K // NZ)
+    ring("hn_", 3, 0, 0, K // NZ)
     for k in range(ROUNDS + 1):
-        ring(f"s{k}n_", 1, 0)
-        ring(f"s{k}f_", 0, 3 if k == 1 else 2)
-        out[f"s{k}_quad_out"] = pltpu.VMEM((2, R, K), F32)
-        out[f"s{k}_quad_in"] = pltpu.VMEM((3, R, K), F32)
-        out[f"s{k}_pair_in"] = pltpu.VMEM((R, K), F32)
-        if k < ROUNDS:
-            out[f"s{k}_yall"] = pltpu.VMEM((NSUB, BLK, K), F32)
-            out[f"s{k}_zall"] = pltpu.VMEM((NZ, 1, BLK, K), F32)
+        for p in range(NH):
+            ring(f"s{k}n{p}_", 1, 0, 0, RH // NZ)
+            ring(f"s{k}f{p}_", 0, 3 if k < ROUNDS else 2, 2, RH // NZ)
+            out[f"s{k}_quad_out{p}"] = pltpu.VMEM((2, RH, K), F32)
+            out[f"s{k}_quad_in{p}"] = pltpu.VMEM((3, RH, K), F32)
+            out[f"s{k}_pair_in{p}"] = pltpu.VMEM((RH, K), F32)
+            if k < ROUNDS:
+                out[f"s{k}_yall{p}"] = pltpu.VMEM((NSUB, RH // NZ, K), F32)
+                out[f"s{k}_zall{p}"] = pltpu.VMEM((NZ, 1, RH // NZ, K), F32)
     return out
 
 
-NSEM = 200
+NSEM = 160 + 140 * NH
 SCRATCH = buffers()
 
 
@@ -149,10 +147,13 @@
 
     far_first = [3, 2, 4, 1, 5, 0, 6]
 
+    def rs_store(tag, mats):
+        for m, mat in enumerate(mats):
+            b[tag + "rs_out"][:, m] = mat.reshape(NZ, mat.shape[0] // NZ, K)
+
     def rs_start(tag, mats):
+        rs_store(tag, mats)
         out = b[tag + "rs_out"]
-        for m, mat in enumerate(mats):
-            out[:, m] = mat.reshape(NZ, BLK, K)
         return [
             send(out.at[lax.rem(z + NZ - d - 1, NZ)], b[tag + "rs_in"].at[d], {"leaf": z_peers[d]})
             for d in far_first
@@ -190,7 +191,8 @@
 
     def ag_finish(name, copies):
         wait(copies)
-        return [b[name][:, i].reshape(R, K) for i in range(b[name].shape[1])]
+        ref = b[name]
+        return [ref[:, i].reshape(NZ * ref.shape[2], K) for i in range(ref.shape[1])]
 
     bhi, blo, gram = b["bhi"], b["blo"], b["gram"]
 
@@ -214,10 +216,10 @@
         return dot3(core[j], split(gram[j, :, cols(l)]), TN)
 
     b["h10"][0] = coupled(1, 0)
-    h1_mats = [coupled(3, 2), coupled(4, 2), coupled(4, 3)]
+    hf_mats = [coupled(4, 3), coupled(5, 3), coupled(5, 4)]
     pl.semaphore_wait(barrier, len(z_peers) + len(y_peers) + len(sub_peers))
     h10_copy = send(b["h10"].at[0], b["h10"].at[1], {"leaf": pair_peer})
-    h1_rs = rs_start("h1_", h1_mats)
+    hf_rs = rs_start("hf_", hf_mats)
 
     def spread(value):
         b["xcat"][:, :R], b["xcat"][:, R:] = split(value)
@@ -248,7 +250,7 @@
     def composed(where, moved):
         hi, lo = split(moved)
         both = dot(jnp.concatenate([hi, lo], axis=0), b["ehi"][where, :])
-        return both[:R] + both[R:] + dot(hi, b["elo"][where, :])
+        return both[: moved.shape[0]] + both[moved.shape[0] :] + dot(hi, b["elo"][where, :])
 
     def block_bases():
         @pl.loop(0, M // 256)
@@ -276,31 +278,31 @@
 
     h = {}
 
-    def level_start(k, q):
+    def level_start(k, p, q):
         u0 = q[:, cols(0)]
         u1 = q[:, cols(1)] - dot3(split(u0), h[1, 0])
-        out = b[f"s{k}_quad_out"]
+        out = b[f"s{k}_quad_out{p}"]
         out[1] = u1
         out[0] = u0
         copies = [
-            send(out.at[1], b[f"s{k}_quad_in"].at[d], {"leaf": quad_peers[d]}) for d in (1, 2, 0)
+            send(out.at[1], b[f"s{k}_quad_in{p}"].at[d], {"leaf": quad_peers[d]}) for d in (1, 2, 0)
         ]
-        return u0, u1, copies + [send(out.at[0], b[f"s{k}_pair_in"], {"leaf": pair_peer})]
-
-    def level_finish(k, q, nb, started):
+        return u0, u1, copies + [send(out.at[0], b[f"s{k}_pair_in{p}"], {"leaf": pair_peer})]
+
+    def level_finish(k, p, q, nb, started):
         u0, u1, copies = started
         wait(copies)
-        quad_in = b[f"s{k}_quad_in"]
-        g0 = u0 + b[f"s{k}_pair_in"][...]
+        quad_in = b[f"s{k}_quad_in{p}"]
+        g0 = u0 + b[f"s{k}_pair_in{p}"][...]
         g1 = (u1 + quad_in[0]) + (quad_in[1] + quad_in[2])
         m01 = jnp.concatenate([dot3(split(g0), core[0], NT), dot3(split(g1), core[1], NT)], axis=1)
         right = slice(2 * K, nb * K)
         both = jnp.concatenate([gram[0, :, right], gram[1, :, right]], axis=0)
         return m01, q[:, right] - dot3(split(m01), split(both))
 
-    def corrected(p, l, u):
-        ul = p[:, cols(l - 2)]
-        for j in range(2, l):
+    def corrected(field, l, u):
+        ul = field[:, cols(l - 2)]
+        for j in sorted(u):
             ul = ul - dot3(u[j], h[l, j])
         u[l] = split(ul)
         return ul
@@ -314,27 +316,55 @@
         leaf_product(b["inv"], put_x)
         return project()
 
-    def moved_of(near, far):
-        return jnp.concatenate(
-            [dot3(split(g), core[l], NT) for l, g in zip((2, 3, 4), (near[0], far[0], far[1]))], axis=1
-        )
-
-    def sub_start(k, block):
-        yall = b[f"s{k}_yall"]
+    def moved_of(level, g):
+        return dot3(split(g), core[level], NT)
+
+    def sub_start(k, p, block):
+        yall = b[f"s{k}_yall{p}"]
         yall[sub] = block
         return [send(yall.at[sub], yall.at[sub], {"sub": peer}) for peer in sub_peers]
 
-    def sub_finish(k, copies):
+    def sub_finish(k, p, copies):
         wait(copies)
-        yall = b[f"s{k}_yall"]
+        yall = b[f"s{k}_yall{p}"]
         hi, lo = split(jnp.concatenate([yall[t] for t in range(NSUB)], axis=1))
-        both = dot(jnp.concatenate([hi, lo], axis=0), b["chi"][...], NT)
-        return ag_start(f"s{k}_zall", [both[:BLK] + both[BLK:] + dot(hi, b["clo"][...], NT)])
-
-    def carry(moved, mixed):
+        if NH == 1:
+            both = dot(jnp.concatenate([hi, lo], axis=0), b["chi"][...], NT)
+            value = both[: RH // NZ] + both[RH // NZ :] + dot(hi, b["clo"][...], NT)
+        else:
+            value = dot(hi, b["chi"][...], NT) + (dot(lo, b["chi"][...], NT) + dot(hi, b["clo"][...], NT))
+        return ag_start(f"s{k}_zall{p}", [value])
+
+    def carry(moved, mixed, further):
         all_moved = jnp.concatenate([moved, -mixed], axis=1)
         b["x"][...] += expand(b["vhi"], b["vlo"], cols(0, NF), all_moved)
-        b["res"][...] += expand(b["dhi"], b["dlo"], cols(0, NF), all_moved)
+        if further:
+            b["res"][...] += expand(b["dhi"], b["dlo"], cols(0, NF), all_moved)
+
+    parts = range(NH)
+
+    def part(value, p):
+        return value[p * RH : (p + 1) * RH]
+
+    def whole(values):
+        return jnp.concatenate(list(values), axis=0)
+
+    def far_reduce(k, rs):
+        totals = [None] * NH
+        ys = [None] * NH
+        for p in parts:
+            totals[p] = rs_finish(f"s{k}f{p}_", rs[p])
+            ys[p] = y_start(f"s{k}f{p}_", totals[p], 1)
+        return totals, ys
+
+    def far_gather(k, totals, ys):
+        subs, ags = [None] * NH, [None] * NH
+        for p in parts:
+            sums = y_finish(f"s{k}f{p}_", totals[p], 1, ys[p])
+            if k < ROUNDS:
+                subs[p] = sub_start(k, p, sums[2])
+            ags[p] = ag_start(f"s{k}f{p}_ag", sums[:2])
+        return subs, ags
 
     l_rhs.wait()
     l_inv.wait()
@@ -343,85 +373,100 @@
     q = project()
     wait([h10_copy])
     h[1, 0] = split(b["h10"][0] + b["h10"][1])
-    started = level_start(0, q)
-    h2_rs = rs_start("h2_", [coupled(5, 2), coupled(5, 3), coupled(5, 4)])
+    q = [part(q, p) for p in parts]
+    started = [level_start(0, p, q[p]) for p in parts]
+    rs_store("hn_", [coupled(3, 2), coupled(4, 2), coupled(5, 2)])
     l_blk.wait()
     block_bases()
     l_coup.wait()
     for t in range(NSUB):
         b["chi"][:, cols(t)], b["clo"][:, cols(t)] = split(b["coup"][t])
-    total = rs_finish("h1_", h1_rs)
-    h1_total = total[2:]
-    h1_y = y_start("h1_", h1_total, 1)
-    h1_near = ag_start("h1_near", [total[0], total[1]])
-    inverse_bases(0, 2)
-    h1_far = ag_start("h1_far", y_finish("h1_", h1_total, 1, h1_y))
-    total = rs_finish("h2_", h2_rs)
-    h2_total = total[1:]
-    h2_y = y_start("h2_", h2_total, 1)
-    h2_near = ag_start("h2_near", [total[0]])
-    inverse_bases(2, 4)
-    m01, p = level_finish(0, q, NB, started)
-    h2_far = ag_start("h2_far", y_finish("h2_", h2_total, 1, h2_y))
-    h[3, 2], h[4, 2] = (split(a) for a in ag_finish("h1_near", h1_near))
-    (h[4, 3],) = (split(a) for a in ag_finish("h1_far", h1_far))
-    u = {}
-    near_rs = rs_start("s0n_", [corrected(p, 2, u)])
-    far_rs = rs_start("s0f_", [corrected(p, 3, u), corrected(p, 4, u)])
-    q = partial(m01)
-    (h[5, 2],) = (split(a) for a in ag_finish("h2_near", h2_near))
-    h[5, 3], h[5, 4] = (split(a) for a in ag_finish("h2_far", h2_far))
-    skel_rs = rs_start("s0y_", [corrected(p, 5, u)])
-    far_total = rs_finish("s0f_", far_rs)
-    far_y = y_start("s0f_", far_total, 1)
-    near_ag = ag_start("s0n_near", [rs_finish("s0n_", near_rs)[0]])
-    project_bases(0, 2)
-    far_ag = ag_start("s0f_far", y_finish("s0f_", far_total, 1, far_y))
-    skel_total = rs_finish("s0y_", skel_rs)
-    skel_y = y_start("s0y_", skel_total, 0)
-    project_bases(2, 4)
-    sub_copies = sub_start(0, y_finish("s0y_", skel_total, 0, skel_y)[0])
-    moved = moved_of(ag_finish("s0n_near", near_ag), ag_finish("s0f_far", far_ag))
-    q = q + composed(cols(0, NF - 1), moved)
-    mixed_copies = sub_finish(0, sub_copies)
-    out_ref[...] = b["x1"][...] - expand(bhi, blo, cols(2, NL), moved)
-
-    (mixed,) = ag_finish("s0_zall", mixed_copies)
-    q = q - composed(cols(NF - 1), mixed)
-    started = level_start(1, q)
-    carry(moved, mixed)
-    m01, p = level_finish(1, q, NB, started)
-    u = {}
-    near_rs = rs_start("s1n_", [corrected(p, 2, u)])
-    far_rs = rs_start("s1f_", [corrected(p, l, u) for l in (3, 4, 5)])
-    q = partial(m01)
-    far_total = rs_finish("s1f_", far_rs)
-    far_y = y_start("s1f_", far_total, 1)
-    near_ag = ag_start("s1n_near", [rs_finish("s1n_", near_rs)[0]])
-    far = y_finish("s1f_", far_total, 1, far_y)
-    sub_copies = sub_start(1, far[2])
-    far_ag = ag_start("s1f_far", far[:2])
-    mixed_copies = sub_finish(1, sub_copies)
-    moved = moved_of(ag_finish("s1n_near", near_ag), ag_finish("s1f_far", far_ag))
-    q = q + composed(cols(0, NF - 1), moved)
-    out_ref[...] += b["x1"][...] - expand(bhi, blo, cols(2, NL), moved)
-
-    (mixed,) = ag_finish("s1_zall", mixed_copies)
-    q = q - composed(cols(NF - 1), mixed)
-    started = level_start(2, q)
-    all_moved = jnp.concatenate([moved, -mixed], axis=1)
-    b["x"][...] += expand(b["vhi"], b["vlo"], cols(0, NF), all_moved)
-    m01, p = level_finish(2, q, NL, started)
-    u = {}
-    near_rs = rs_start("s2n_", [corrected(p, 2, u)])
-    far_rs = rs_start("s2f_", [corrected(p, l, u) for l in (3, 4)])
-    out_ref[...] += b["x"][...] - expand(bhi, blo, cols(0, 2), m01)
-    far_total = rs_finish("s2f_", far_rs)
-    far_y = y_start("s2f_", far_total, 1)
-    near_ag = ag_start("s2n_near", [rs_finish("s2n_", near_rs)[0]])
-    far_ag = ag_start("s2f_far", y_finish("s2f_", far_total, 1, far_y))
-    moved = moved_of(ag_finish("s2n_near", near_ag), ag_finish("s2f_far", far_ag))
-    out_ref[...] -= expand(bhi, blo, cols(2, NL), moved)
+    hf_total = rs_finish("hf_", hf_rs)
+    hf_y = y_start("hf_", hf_total, 2)
+    fields, m01s, near_rs = [], [], []
+    for p in parts:
+        m01, field = level_finish(0, p, q[p], NB, started[p])
+        m01s.append(m01)
+        fields.append(field)
+        near_rs.append(rs_start(f"s0n{p}_", [field[:, cols(0)]]))
+    hf_ag = ag_start("hf_ag", y_finish("hf_", hf_total, 2, hf_y))
+    inverse_bases(0, 3)
+    near_ag = [ag_start(f"s0n{p}_ag", [rs_finish(f"s0n{p}_", near_rs[p])[0]]) for p in parts]
+    hn_rs = rs_start("hn_", [])
+    inverse_bases(3, 4)
+    hf = ag_finish("hf_ag", hf_ag)
+    for i, pair in enumerate([(4, 3), (5, 3), (5, 4)]):
+        h[pair] = split(hf[i])
+    m2s, far_rs = [], []
+    for p in parts:
+        (g2,) = ag_finish(f"s0n{p}_ag", near_ag[p])
+        m2s.append(moved_of(2, g2))
+        right = slice(3 * K, NB * K)
+        field = fields[p][:, K:] - dot3(split(m2s[p]), split(gram[2, :, right]))
+        field = jnp.concatenate([field[:, :K], field], axis=1)
+        u = {}
+        far_rs.append(rs_start(f"s0f{p}_", [corrected(field, l, u) for l in (3, 4, 5)]))
+    q = partial(whole(m01s))
+    totals, ys = far_reduce(0, far_rs)
+    hn_total = rs_finish("hn_", hn_rs)
+    hn_ag = ag_start("hn_ag", [hn_total[i] for i in range(3)])
+    project_bases(0, 1)
+    subs, far_ags = far_gather(0, totals, ys)
+    project_bases(1, 4)
+    hn = ag_finish("hn_ag", hn_ag)
+    for i, pair in enumerate([(3, 2), (4, 2), (5, 2)]):
+        h[pair] = split(hn[i])
+
+    for k in range(ROUNDS):
+        zs = [sub_finish(k, p, subs[p]) for p in parts]
+        qs, moves = [], []
+        for p in parts:
+            if k:
+                m2 = moved_of(2, ag_finish(f"s{k}n{p}_ag", near_ag[p])[0])
+            else:
+                m2 = m2s[p]
+            g3, g4 = ag_finish(f"s{k}f{p}_ag", far_ags[p])
+            moves.append(jnp.concatenate([m2, moved_of(3, g3), moved_of(4, g4)], axis=1))
+            qs.append(part(q, p) + composed(cols(0, NF - 1), moves[p]))
+        moved = whole(moves)
+        step = b["x1"][...] - expand(bhi, blo, cols(2, NL), moved)
+        if k == 0:
+            out_ref[...] = step
+        else:
+            out_ref[...] += step
+
+        nb = NB if k + 1 < ROUNDS else NL
+        mixes, started = [], []
+        for p in parts:
+            (mixed,) = ag_finish(f"s{k}_zall{p}", zs[p])
+            mixes.append(mixed)
+            qs[p] = qs[p] - composed(cols(NF - 1), mixed)
+            started.append(level_start(k + 1, p, qs[p]))
+        carry(moved, whole(mixes), k + 1 < ROUNDS)
+        m01s, near_rs, far_rs = [], [], []
+        for p in parts:
+            m01, field = level_finish(k + 1, p, qs[p], nb, started[p])
+            m01s.append(m01)
+            u = {}
+            near_rs.append(rs_start(f"s{k + 1}n{p}_", [corrected(field, 2, u)]))
+            far_rs.append(rs_start(f"s{k + 1}f{p}_", [corrected(field, l, u) for l in range(3, nb)]))
+        m01 = whole(m01s)
+        if k + 1 < ROUNDS:
+            q = partial(m01)
+        else:
+            out_ref[...] += b["x"][...] - expand(bhi, blo, cols(0, 2), m01)
+        totals, ys = far_reduce(k + 1, far_rs)
+        near_ag = [ag_start(f"s{k + 1}n{p}_ag", [rs_finish(f"s{k + 1}n{p}_", near_rs[p])[0]]) for p in parts]
+        subs, far_ags = far_gather(k + 1, totals, ys)
+
+    moves = []
+    for p in parts:
+        g2 = ag_finish(f"s{ROUNDS}n{p}_ag", near_ag[p])[0]
+        g3, g4 = ag_finish(f"s{ROUNDS}f{p}_ag", far_ags[p])
+        moves.append(
+            jnp.concatenate([moved_of(l, g) for l, g in ((2, g2), (3, g3), (4, g4))], axis=1)
+        )
+    out_ref[...] -= expand(bhi, blo, cols(2, NL), whole(moves))
 
     for copy in sent:
         copy.wait_send()

time: 113 us -> 111 us (0.982)
  Pallas kernels: 111 us -> 109 us
    pallas_call x1, Pallas kernels: 111 us -> 109 us  [body(): pl.pallas_call(kernel, out_shape=jax.ShapeDtypeStruct((M, R), F32), in_sp...]
where the time goes in v3:
time: 111 us
  Pallas kernels  109 us (98%)
  local copies, waits for them, and re-layouts  1.87 us (2%)
    pallas_call x1, Pallas kernels, body(): pl.pallas_call(kernel, out_shape=jax.ShapeDtypeStruct((M, R), F32), in_sp...  109 us

profile of v3, /device:TPU:6, one launch (start us, length us, event | category | flops | bytes accessed | tf_op | source)
XLA Modules:
  0.0 111.2 jit_solution(12593789888614832687)
XLA Ops:
  0.0 109.3 %ridge_rounds.1 = f32[1024,128]{1,0:T(8,128)} custom-call(f32[1024,128]{1,0:T(8,128)} %bitcast.12, bf16[1024,1024]{1,0:T(8,128)(2,1)} %bitcast.10, bf16[1024,1024]{1,0:T(8,128)(2,1)} %bitcast.11, f32[5,1024,128]{2,1,0:T(8,128)} %bitcast.9, f32[5,128,128]{2,1,0:T(8,128)} %bitcast.15, f32[1024,128]{1,0:T(8,128)} %bitcast.13, f32[8,128,128]{2,1,0:T(8,128)} %bitcast.14), custom_call_target="tpu_custom_call" | custom-call | flops 8000000000 | bytes 10000000 | tf_op jit(solution)/shard_map/ridge_rounds/pallas_call | solution.py:477
  109.3 1.9 %copy.9 = f32[1,1,1024,128]{3,2,1,0:T(8,128)} copy(f32[1,1,1024,128]{3,2,1,0:T(8,128)} %bitcast.8) | data formatting | bytes 1048576

commit v4 on v3

--- a/solution.py
+++ b/solution.py
@@ -74,6 +74,9 @@
 
     ring("hf_", 0, 3, 3, K // NZ)
     ring("hn_", 3, 0, 0, K // NZ)
+    out["e_out"] = pltpu.VMEM((2, K, K), F32)
+    out["e_quad"] = pltpu.VMEM((3, K, K), F32)
+    out["e_pair"] = pltpu.VMEM((K, K), F32)
     for k in range(ROUNDS + 1):
         for p in range(NH):
             ring(f"s{k}n{p}_", 1, 0, 0, RH // NZ)
@@ -289,12 +292,14 @@
         ]
         return u0, u1, copies + [send(out.at[0], b[f"s{k}_pair_in{p}"], {"leaf": pair_peer})]
 
-    def level_finish(k, p, q, nb, started):
+    def level_finish(k, p, q, nb, started, late=None):
         u0, u1, copies = started
         wait(copies)
         quad_in = b[f"s{k}_quad_in{p}"]
         g0 = u0 + b[f"s{k}_pair_in{p}"][...]
         g1 = (u1 + quad_in[0]) + (quad_in[1] + quad_in[2])
+        if late is not None:
+            g0, g1 = g0 - late[:, cols(0)], g1 - late[:, cols(1)]
         m01 = jnp.concatenate([dot3(split(g0), core[0], NT), dot3(split(g1), core[1], NT)], axis=1)
         right = slice(2 * K, nb * K)
         both = jnp.concatenate([gram[0, :, right], gram[1, :, right]], axis=0)
@@ -394,6 +399,12 @@
     near_ag = [ag_start(f"s0n{p}_ag", [rs_finish(f"s0n{p}_", near_rs[p])[0]]) for p in parts]
     hn_rs = rs_start("hn_", [])
     inverse_bases(3, 4)
+    project_bases(NF - 1, NF)
+    skel = cols(NF - 1)
+    e0 = b["ehi"][skel, cols(0)], b["elo"][skel, cols(0)]
+    e_out = b["e_out"]
+    e_out[0] = e0[0].astype(F32) + e0[1].astype(F32)
+    e_out[1] = b["ehi"][skel, cols(1)].astype(F32) + b["elo"][skel, cols(1)].astype(F32) - dot3(e0, h[1, 0])
     hf = ag_finish("hf_ag", hf_ag)
     for i, pair in enumerate([(4, 3), (5, 3), (5, 4)]):
         h[pair] = split(hf[i])
@@ -410,9 +421,11 @@
     totals, ys = far_reduce(0, far_rs)
     hn_total = rs_finish("hn_", hn_rs)
     hn_ag = ag_start("hn_ag", [hn_total[i] for i in range(3)])
+    e_copies = [send(e_out.at[1], b["e_quad"].at[d], {"leaf": quad_peers[d]}) for d in (1, 2, 0)]
+    e_copies.append(send(e_out.at[0], b["e_pair"], {"leaf": pair_peer}))
     project_bases(0, 1)
     subs, far_ags = far_gather(0, totals, ys)
-    project_bases(1, 4)
+    project_bases(1, NF - 1)
     hn = ag_finish("hn_ag", hn_ag)
     for i, pair in enumerate([(3, 2), (4, 2), (5, 2)]):
         h[pair] = split(hn[i])
@@ -428,24 +441,31 @@
             g3, g4 = ag_finish(f"s{k}f{p}_ag", far_ags[p])
             moves.append(jnp.concatenate([m2, moved_of(3, g3), moved_of(4, g4)], axis=1))
             qs.append(part(q, p) + composed(cols(0, NF - 1), moves[p]))
+        nb = NB if k + 1 < ROUNDS else NL
+        started = [level_start(k + 1, p, qs[p]) for p in parts]
         moved = whole(moves)
         step = b["x1"][...] - expand(bhi, blo, cols(2, NL), moved)
         if k == 0:
             out_ref[...] = step
+            wait(e_copies)
+            e_quad = b["e_quad"]
+            shared = split(
+                jnp.concatenate(
+                    [e_out[0] + b["e_pair"][...], (e_out[1] + e_quad[0]) + (e_quad[1] + e_quad[2])], axis=1
+                )
+            )
         else:
             out_ref[...] += step
-
-        nb = NB if k + 1 < ROUNDS else NL
-        mixes, started = [], []
+        mixes, lates = [], []
         for p in parts:
             (mixed,) = ag_finish(f"s{k}_zall{p}", zs[p])
             mixes.append(mixed)
             qs[p] = qs[p] - composed(cols(NF - 1), mixed)
-            started.append(level_start(k + 1, p, qs[p]))
+            lates.append(dot3(split(mixed), shared))
         carry(moved, whole(mixes), k + 1 < ROUNDS)
         m01s, near_rs, far_rs = [], [], []
         for p in parts:
-            m01, field = level_finish(k + 1, p, qs[p], nb, started[p])
+            m01, field = level_finish(k + 1, p, qs[p], nb, started[p], lates[p])
             m01s.append(m01)
             u = {}
             near_rs.append(rs_start(f"s{k + 1}n{p}_", [corrected(field, 2, u)]))

time: 111 us -> 115 us (1.036); the launches traced: 111 us -> 113 us
  Pallas kernels: 109 us -> 111 us
    pallas_call x1, Pallas kernels: 109 us -> 111 us  [body(): pl.pallas_call(kernel, out_shape=jax.ShapeDtypeStruct((M, R), F32), in_sp...]
where the time goes in v4:
time: 115 us; the launch traced here: 113 us
  Pallas kernels  111 us (97%)
  local copies, waits for them, and re-layouts  1.87 us (2%)
    pallas_call x1, Pallas kernels, body(): pl.pallas_call(kernel, out_shape=jax.ShapeDtypeStruct((M, R), F32), in_sp...  111 us

profile of v4, /device:TPU:6, one launch (start us, length us, event | category | flops | bytes accessed | tf_op | source)
XLA Modules:
  0.0 112.8 jit_solution(5887476423279935666)
XLA Ops:
  0.0 110.9 %ridge_rounds.1 = f32[1024,128]{1,0:T(8,128)} custom-call(f32[1024,128]{1,0:T(8,128)} %bitcast.12, bf16[1024,1024]{1,0:T(8,128)(2,1)} %bitcast.10, bf16[1024,1024]{1,0:T(8,128)(2,1)} %bitcast.11, f32[5,1024,128]{2,1,0:T(8,128)} %bitcast.9, f32[5,128,128]{2,1,0:T(8,128)} %bitcast.15, f32[1024,128]{1,0:T(8,128)} %bitcast.13, f32[8,128,128]{2,1,0:T(8,128)} %bitcast.14), custom_call_target="tpu_custom_call" | custom-call | flops 8000000000 | bytes 10000000 | tf_op jit(solution)/shard_map/ridge_rounds/pallas_call | solution.py:497
  111.0 1.9 %copy.9 = f32[1,1,1024,128]{3,2,1,0:T(8,128)} copy(f32[1,1,1024,128]{3,2,1,0:T(8,128)} %bitcast.8) | data formatting | bytes 1048576

commit v5 on v3

--- a/solution.py
+++ b/solution.py
@@ -145,6 +145,13 @@
         for copy in copies:
             copy.wait_recv()
 
+    drained = []
+
+    def drain(recent):
+        for copy in sent[len(drained) : len(sent) - recent]:
+            copy.wait_send()
+            drained.append(copy)
+
     far_first = [3, 2, 4, 1, 5, 0, 6]
 
     def rs_store(tag, mats):
@@ -350,6 +357,7 @@
         return jnp.concatenate(list(values), axis=0)
 
     def far_reduce(k, rs):
+        drain(14 * NH)
         totals = [None] * NH
         ys = [None] * NH
         for p in parts:
@@ -358,6 +366,7 @@
         return totals, ys
 
     def far_gather(k, totals, ys):
+        drain(17 * NH)
         subs, ags = [None] * NH, [None] * NH
         for p in parts:
             sums = y_finish(f"s{k}f{p}_", totals[p], 1, ys[p])
@@ -459,6 +468,7 @@
         near_ag = [ag_start(f"s{k + 1}n{p}_ag", [rs_finish(f"s{k + 1}n{p}_", near_rs[p])[0]]) for p in parts]
         subs, far_ags = far_gather(k + 1, totals, ys)
 
+    drain(17 * NH)
     moves = []
     for p in parts:
         g2 = ag_finish(f"s{ROUNDS}n{p}_ag", near_ag[p])[0]
@@ -468,8 +478,7 @@
         )
     out_ref[...] -= expand(bhi, blo, cols(2, NL), whole(moves))
 
-    for copy in sent:
-        copy.wait_send()
+    drain(0)
 
 
 def body(rhs, leaf_block, leaf_inverse, level_basis, level_core, skeleton_basis, coupling):

time: 111 us -> 111 us (level)
  no operation moved by 1% of the time
where the time goes in v5:
time: 111 us
  Pallas kernels  109 us (98%)
  local copies, waits for them, and re-layouts  1.87 us (2%)
    pallas_call x1, Pallas kernels, body(): pl.pallas_call(kernel, out_shape=jax.ShapeDtypeStruct((M, R), F32), in_sp...  109 us

profile of v5, /device:TPU:6, one launch (start us, length us, event | category | flops | bytes accessed | tf_op | source)
XLA Modules:
  0.0 111.0 jit_solution(5150011399058041517)
XLA Ops:
  0.0 109.1 %ridge_rounds.1 = f32[1024,128]{1,0:T(8,128)} custom-call(f32[1024,128]{1,0:T(8,128)} %bitcast.12, bf16[1024,1024]{1,0:T(8,128)(2,1)} %bitcast.10, bf16[1024,1024]{1,0:T(8,128)(2,1)} %bitcast.11, f32[5,1024,128]{2,1,0:T(8,128)} %bitcast.9, f32[5,128,128]{2,1,0:T(8,128)} %bitcast.15, f32[1024,128]{1,0:T(8,128)} %bitcast.13, f32[8,128,128]{2,1,0:T(8,128)} %bitcast.14), custom_call_target="tpu_custom_call" | custom-call | flops 8000000000 | bytes 10000000 | tf_op jit(solution)/shard_map/ridge_rounds/pallas_call | solution.py:486
  109.1 1.9 %copy.9 = f32[1,1,1024,128]{3,2,1,0:T(8,128)} copy(f32[1,1,1024,128]{3,2,1,0:T(8,128)} %bitcast.8) | data formatting | bytes 1048576
